TPU v7x, 128 devices: a whole 4x4x4 slice. The times are simulated.
128 devices in a mesh: prompt: 16 (over z, y), ctx: 8 (over x, core).
Axes of the slice: x: 4, y: 4, z: 4, core: 2. Of those that a mesh axis runs over, the one named last changes fastest.
Arguments:
- probe_vectors: bfloat16 [256, 4, 8192], P('prompt', None, 'ctx'), may hold values from -9.5 to 9.5
- tail_memory_tensor: bfloat16 [256, 512, 2048], P('prompt', None, 'ctx'), may hold values from -6 to 6
- common_lead_memory: bfloat16 [16, 32768, 2048], P('prompt', 'ctx'), may hold values from -6 to 6
- active_rollouts: int32 [16], replicated, may hold values from 4 to 8, as said below
- holder_map: int32 [128], replicated, may hold values from 0 to 15, as said below
- tail_fill_extent: int32 [256], P('prompt'), may hold values from 4 to 512, as said below
Outputs:
- attended: bfloat16 [256, 4, 8192], P('prompt', None, 'ctx')
- log_mass: float32 [256, 4, 64], P('prompt', None, 'ctx')
Inputs may be any that keep to these rules, and one draw needn't show every extreme that they name: `active_rollouts`: every prompt keeps at least 4 samples; some prompt keeps all. `holder_map`: each owner index holds at most 16 live samples and at most 4 live samples of one prompt; in every draw some index holds exactly 16 live samples with exactly 4 of one prompt. `tail_fill_extent`: some slot has all 512 positions filled.
All inputs are finite; a program needn't handle non-finite values.
Results may differ from a plain program's by a relative error of at most 0.0057.
Values may be sent and summed in bfloat16 or wider, within the bound.
A program may use at most 192 MiB of HBM per device.

v0:
```python
import jax
import jax.numpy as jnp
from jax import lax
from jax.sharding import PartitionSpec as P

QUERY_HEADS = 64
KEY_VALUE_HEADS = 8
HEAD_SIZE = 128
SAMPLE_COUNT = 8
CAP = 4
OWNER_SLOTS = 16


def dispatch_layout(active_rollouts, holder_map):
    sample_ids = jnp.arange(holder_map.shape[0], dtype=jnp.int32)
    request_number = sample_ids // SAMPLE_COUNT
    within_offset = sample_ids % SAMPLE_COUNT
    request_finder = jnp.arange(active_rollouts.shape[0], dtype=jnp.int32)
    surviving_total = jnp.sum(
        jnp.where(request_number[:, None] == request_finder[None, :], active_rollouts[None, :], 0),
        axis=1,
    )
    active_marker = within_offset < surviving_total
    earlier = (
        active_marker[:, None]
        & (holder_map[:, None] == holder_map[None, :])
        & (sample_ids[:, None] < sample_ids[None, :])
    )
    tail_bucket_number = jnp.sum(earlier.astype(jnp.int32), axis=0)
    same_prompt = earlier & (request_number[:, None] == request_number[None, :])
    worker_ordinal = jnp.sum(same_prompt.astype(jnp.int32), axis=0)
    return (request_number, within_offset, active_marker, tail_bucket_number, worker_ordinal)


def prefix_attention(query_head_block, shard_rows):
    head_count = shard_rows.shape[1]
    query_view = query_head_block.reshape(query_head_block.shape[0], head_count, -1, HEAD_SIZE)
    scores = jnp.einsum(
        "rhgd,nhd->hrgn", query_view, shard_rows[:, :, 0], preferred_element_type=jnp.float32
    ) * HEAD_SIZE ** (-0.5)
    highest = jnp.max(scores, axis=-1)
    weights = jnp.exp(scores - highest[..., None])
    totals = jnp.sum(weights, axis=-1)
    values = jnp.einsum(
        "hrgn,nhd->hrgd",
        weights.astype(jnp.bfloat16),
        shard_rows[:, :, 1],
        preferred_element_type=jnp.float32,
    )
    return ((values / totals[..., None]).astype(jnp.bfloat16), highest + jnp.log(totals))


def merge_shards(values, lse):
    highest = jnp.max(lse, axis=1, keepdims=True)
    weights = jnp.exp(lse - highest)
    totals = jnp.sum(weights, axis=1)
    merged = jnp.sum(weights[..., None] * values, axis=1) / totals[..., None]
    return (merged, highest[:, 0] + jnp.log(totals))


def suffix_attention(query_block, cache_block, lengths):
    slot_count, decode_step_count = (query_block.shape[0], query_block.shape[1])
    key_span = cache_block.shape[1]
    head_count = cache_block.shape[2] // (2 * HEAD_SIZE)
    group_width = query_block.shape[2] // (head_count * HEAD_SIZE)
    query_view = query_block.reshape(
        slot_count, decode_step_count, head_count, group_width, HEAD_SIZE
    )
    cache_view = cache_block.reshape(slot_count, key_span, head_count, 2, HEAD_SIZE)
    scores = jnp.einsum(
        "sthgd,smhd->sthgm", query_view, cache_view[:, :, :, 0], preferred_element_type=jnp.float32
    ) * HEAD_SIZE ** (-0.5)
    limits = (
        lengths[:, None]
        - decode_step_count
        + 1
        + jnp.arange(decode_step_count, dtype=jnp.int32)[None, :]
    )
    visible = jnp.arange(key_span, dtype=jnp.int32)[None, None, :] < limits[:, :, None]
    masked = jnp.where(visible[:, :, None, None, :], scores, -1e30)
    highest = jnp.max(masked, axis=-1)
    weights = jnp.exp(masked - highest[..., None])
    totals = jnp.sum(weights, axis=-1)
    values = jnp.einsum(
        "sthgm,smhd->sthgd",
        weights.astype(jnp.bfloat16),
        cache_view[:, :, :, 1],
        preferred_element_type=jnp.float32,
    )
    return (values / totals[..., None], highest + jnp.log(totals))


def combine_parts(prefix_output, prefix_log_sum, suffix_output, suffix_log_sum, slot_live):
    log_mass = jnp.logaddexp(prefix_log_sum, suffix_log_sum)
    mixed = (
        jnp.exp(prefix_log_sum - log_mass)[..., None] * prefix_output
        + jnp.exp(suffix_log_sum - log_mass)[..., None] * suffix_output
    )
    live_mask = slot_live[:, None, None, None]
    attended = (mixed * live_mask[..., None]).astype(jnp.bfloat16)
    row_count, decode_step_count = (mixed.shape[0], mixed.shape[1])
    return (
        attended.reshape(row_count, decode_step_count, -1),
        (log_mass * live_mask).reshape(row_count, decode_step_count, -1),
    )


def per_device(
    probe_vectors,
    tail_memory_tensor,
    common_lead_memory,
    active_rollouts,
    holder_map,
    tail_fill_extent,
):
    group_width = QUERY_HEADS // KEY_VALUE_HEADS
    row_count = lax.axis_size("prompt")
    own_row = lax.axis_index("prompt")
    ctx_index = lax.axis_index("ctx")
    slot_count, decode_step_count, head_width = probe_vectors.shape
    local_heads = tail_memory_tensor.shape[2] // (2 * HEAD_SIZE)
    request_number, within_offset, active_marker, tail_bucket_number, worker_ordinal = (
        dispatch_layout(active_rollouts, holder_map)
    )
    positions = jnp.arange(row_count * CAP, dtype=jnp.int32)
    slot_table = jnp.arange(OWNER_SLOTS, dtype=jnp.int32)
    sample_table = jnp.arange(SAMPLE_COUNT, dtype=jnp.int32)
    owned_here = active_marker & (holder_map == own_row)
    outgoing = (
        owned_here[:, None]
        & ((request_number * CAP + worker_ordinal)[:, None] == positions[None, :])
    ).astype(jnp.float32)
    in_slot = (tail_bucket_number[:, None] == slot_table[None, :]).astype(jnp.float32)
    send_table = jnp.dot(outgoing.T, in_slot, precision=lax.Precision.HIGHEST)
    prompt_live = active_marker & (request_number == own_row)
    as_sample = (prompt_live[:, None] & (within_offset[:, None] == sample_table[None, :])).astype(
        jnp.float32
    )
    from_pos = ((holder_map * CAP + worker_ordinal)[:, None] == positions[None, :]).astype(
        jnp.float32
    )
    take_table = jnp.dot(as_sample.T, from_pos, precision=lax.Precision.HIGHEST)
    send_bits = send_table.astype(jnp.bfloat16)
    take_bits = take_table.astype(jnp.bfloat16)
    all_heads = lax.all_gather(probe_vectors, "ctx", axis=2, tiled=True)
    packed = jnp.dot(
        send_bits, all_heads.reshape(slot_count, -1), preferred_element_type=jnp.float32
    ).astype(jnp.bfloat16)
    packed = packed.reshape(row_count, CAP, decode_step_count, QUERY_HEADS * HEAD_SIZE)
    arrived = lax.all_to_all(packed, "prompt", split_axis=0, concat_axis=0, tiled=True)
    complete_query_rows = jnp.dot(
        take_bits, arrived.reshape(row_count * CAP, -1), preferred_element_type=jnp.float32
    ).astype(jnp.bfloat16)
    complete_query_rows = complete_query_rows.reshape(
        SAMPLE_COUNT, decode_step_count, QUERY_HEADS * HEAD_SIZE
    )
    prefix_row_block = common_lead_memory.reshape(-1, KEY_VALUE_HEADS, 2, HEAD_SIZE)
    query_head_block = complete_query_rows.reshape(
        SAMPLE_COUNT * decode_step_count, KEY_VALUE_HEADS, group_width * HEAD_SIZE
    )
    part_vals, part_lse = prefix_attention(query_head_block, prefix_row_block)
    every_vals = lax.all_gather(part_vals[None], "ctx", axis=0, tiled=True)
    every_lse = lax.all_gather(part_lse[None], "ctx", axis=0, tiled=True)
    every_vals = lax.dynamic_slice_in_dim(
        jnp.moveaxis(every_vals, 0, 1), ctx_index * local_heads, local_heads, 0
    )
    every_lse = lax.dynamic_slice_in_dim(
        jnp.moveaxis(every_lse, 0, 1), ctx_index * local_heads, local_heads, 0
    )
    own_vals, own_lse = merge_shards(every_vals.astype(jnp.float32), every_lse)
    prefix_out = own_vals.astype(jnp.bfloat16).reshape(
        local_heads, SAMPLE_COUNT, decode_step_count, group_width * HEAD_SIZE
    )
    prefix_log_sum = own_lse.reshape(local_heads, SAMPLE_COUNT, decode_step_count, group_width)
    back_vals = jnp.einsum(
        "jk,hjtx->khtx", take_bits, prefix_out, preferred_element_type=jnp.float32
    ).astype(jnp.bfloat16)
    back_lse = jnp.einsum(
        "jk,hjtg->khtg", take_table, prefix_log_sum, precision=lax.Precision.HIGHEST
    )
    back_vals = back_vals.reshape(
        row_count, CAP, local_heads, decode_step_count, group_width * HEAD_SIZE
    )
    back_lse = back_lse.reshape(row_count, CAP, local_heads, decode_step_count, group_width)
    home_vals = lax.all_to_all(back_vals, "prompt", split_axis=0, concat_axis=0, tiled=True)
    home_lse = lax.all_to_all(back_lse, "prompt", split_axis=0, concat_axis=0, tiled=True)
    slot_output = jnp.einsum(
        "ks,khtx->sthx",
        send_bits,
        home_vals.reshape(row_count * CAP, local_heads, decode_step_count, -1),
        preferred_element_type=jnp.float32,
    )
    slot_log_sum = jnp.einsum(
        "ks,khtg->sthg",
        send_table,
        home_lse.reshape(row_count * CAP, local_heads, decode_step_count, -1),
        precision=lax.Precision.HIGHEST,
    )
    slot_output = slot_output.reshape(
        slot_count, decode_step_count, local_heads, group_width, HEAD_SIZE
    )
    slot_live = jnp.sum(send_table, axis=0)
    suffix_output, suffix_log_sum = suffix_attention(
        probe_vectors, tail_memory_tensor, tail_fill_extent
    )
    attended, log_mass = combine_parts(
        slot_output, slot_log_sum, suffix_output, suffix_log_sum, slot_live
    )
    return (attended, log_mass)


def solution(mesh):
    return jax.shard_map(
        per_device,
        mesh=mesh,
        in_specs=(
            P("prompt", None, "ctx"),
            P("prompt", None, "ctx"),
            P("prompt", "ctx", None),
            P(),
            P(),
            P("prompt"),
        ),
        out_specs=(P("prompt", None, "ctx"), P("prompt", None, "ctx")),
        check_vma=False,
    )
```

profile of v0, /device:TPU:1, one launch (start us, length us, event | category | flops | bytes accessed | tf_op | source)
XLA Modules:
  0.0 235.6 jit_solution(2492432707652844326)
XLA Ops:
  9.3 0.9 convert_reduce_fusion.1
  11.2 25.5 %all-gather.5.cloned.1.call-done = bf16[16,4,8192]{2,1,0:T(4,128)(2,1)} async-done(((bf16[16,4,1024]{2,1,0:T(4,128)(2,1)}), bf16[16,4,8192]{2,1,0:T(4,128)(2,1)}) %all-gather.5.cloned.1.call-update) | async-done | bytes 1048592 | tf_op jit(solution)/shard_map/all_gather | solution.py:145
  36.7 1.8 copy.174
  38.5 3.2 %convolution_convert_fusion = bf16[64,32768]{1,0:T(8,128)(2,1)} fusion(bf16[16,32768]{1,0:T(8,128)(2,1)S(1)} %bitcast.199, f32[64,16]{0,1:T(8,128)S(1)} %get-tuple-element.17), kind=kOutput, calls=%fused_computation | convolution fusion | flops 69207040 | bytes 5246976 | tf_op jit(solution)/shard_map/dot_general | solution.py:146
  41.7 7.8 %reshape.309 = bf16[16,4,4,8192]{3,2,1,0:T(4,128)(2,1)} reshape(bf16[64,32768]{1,0:T(8,128)(2,1)} %convolution_convert_fusion) | data formatting | bytes 8388608 | tf_op jit(solution)/shard_map/reshape | solution.py:149
  49.6 6.7 %all-to-all-start = ((bf16[16,4,4,8192]{3,2,1,0:T(4,128)(2,1)}), bf16[16,4,4,8192]{3,2,1,0:T(4,128)(2,1)}, u32[]{:S(2)}, u32[]{:S(2)}) async-start(bf16[16,4,4,8192]{3,2,1,0:T(4,128)(2,1)} %reshape.309), calls=%async_computation | async-start | bytes 8388608 | tf_op jit(solution)/shard_map/all_to_all | solution.py:150
  56.6 20.9 %copy.134 = bf16[1,4096,2048]{1,2,0:T(8,128)(2,1)} copy(bf16[1,4096,2048]{2,1,0:T(8,128)(2,1)} %param.8) | data formatting | bytes 33554432 | tf_op args[2]
  77.7 41.5 %all-to-all-done = bf16[16,4,4,8192]{3,2,1,0:T(4,128)(2,1)} async-done(((bf16[16,4,4,8192]{3,2,1,0:T(4,128)(2,1)}), bf16[16,4,4,8192]{3,2,1,0:T(4,128)(2,1)}, u32[]{:S(2)}, u32[]{:S(2)}) %all-to-all-start) | async-done | bytes 4194336 | tf_op jit(solution)/shard_map/all_to_all | solution.py:150
  119.2 4.6 %copy.175 = bf16[8,8,4,8192]{3,1,2,0:T(8,128)(2,1)S(1)} copy(bf16[8,8,4,8192]{3,2,1,0:T(4,128)(2,1)} %bitcast.64) | data formatting | bytes 8388608
  124.8 16.6 %multiply_reduce_fusion = (f32[8,32,8]{2,1,0:T(8,128)S(1)}, f32[8,32,8,4096]{3,2,1,0:T(8,128)}) fusion(bf16[4096,8,2,128]{0,3,2,1:T(8,128)(2,1)} %bitcast.196, bf16[32,8,8,128]{3,2,1,0:T(8,128)(2,1)S(1)} %reshape_reshape_reshape.3), kind=kOutput, calls=%fused_computation.3 | convolution fusion | flops 2164258816 | bytes 42475520 | tf_op jit(solution)/shard_map/rhgd,nhd->hrgn/dot_general | solution.py:38
  141.4 14.0 %fusion.1 = f32[8,32,8]{2,1,0:T(8,128)S(1)} fusion(f32[8,32,8,4096]{3,2,1,0:T(8,128)} %get-tuple-element.15, f32[8,32,8]{2,1,0:T(8,128)S(1)} %get-tuple-element.14), kind=kLoop, calls=%fused_computation.5 | loop fusion | flops 25163776 | bytes 33570816 | tf_op jit(solution)/shard_map/reduce_sum | solution.py:43
  155.4 17.5 %fusion.16 = bf16[8,32,8,128]{3,2,1,0:T(8,128)(2,1)} fusion(bf16[4096,8,2,128]{0,3,2,1:T(8,128)(2,1)} %bitcast.197, f32[8,32,8,4096]{3,2,1,0:T(8,128)} %get-tuple-element.15, f32[8,32,8]{2,1,0:T(8,128)S(1)} %get-tuple-element.14, f32[8,32,8]{2,1,0:T(8,128)S(1)} %fusion.1), kind=kOutput, calls=%fused_computation.22 | convolution fusion | flops 2173173760 | bytes 42483712 | tf_op jit(solution)/shard_map/hrgn,nhd->hrgd/dot_general | solution.py:44
  173.0 6.4 %copy.145 = bf16[16,512,256]{1,2,0:T(8,128)(2,1)} copy(bf16[16,512,256]{2,1,0:T(8,128)(2,1)} %param.7) | data formatting | bytes 8388608 | tf_op args[1]
  179.9 14.4 %all-gather = f32[64,32,8]{1,2,0:T(8,128)S(1)} all-gather(f32[8,32,8]{1,2,0:T(8,128)S(1)} %log_add_fusion), channel_id=2, replica_groups=mesh['prompt'=16,'ctx'=8] {'ctx'}, dimensions={0}, use_global_device_ids=true | all-gather | bytes 73728 | tf_op jit(solution)/shard_map/all_gather | solution.py:163
  195.2 0.8 reshape.335
  196.0 4.8 %all-to-all-start.1 = ((f32[16,1,128]{2,1,0:T(1,128)}), f32[16,1,128]{2,1,0:T(1,128)S(1)}, u32[]{:S(2)}, u32[]{:S(2)}) async-start(f32[16,1,128]{2,1,0:T(1,128)} %reshape.335), calls=%async_computation.1 | async-start | bytes 16384 | tf_op jit(solution)/shard_map/all_to_all | solution.py:186
  200.8 4.2 %all-gather.7.cloned.1.call-done = bf16[64,32,8,128]{3,2,1,0:T(8,128)(2,1)} async-done(((bf16[8,32,8,128]{3,2,1,0:T(8,128)(2,1)}), bf16[64,32,8,128]{3,2,1,0:T(8,128)(2,1)}) %all-gather.7.cloned.1.call-update) | async-done | bytes 4194320 | tf_op jit(solution)/shard_map/all_gather | solution.py:162
  205.0 1.4 fusion.25
  207.1 1.0 copy.154
  208.1 6.1 %all-to-all-start.2 = ((bf16[16,4,1,4,1024]{4,1,3,2,0:T(4,128)(2,1)}), bf16[16,4,1,4,1024]{4,1,3,2,0:T(4,128)(2,1)S(1)}, u32[]{:S(2)}, u32[]{:S(2)}) async-start(bf16[16,4,1,4,1024]{4,1,3,2,0:T(4,128)(2,1)} %copy.154), calls=%async_computation.2 | async-start | bytes 1048576 | tf_op jit(solution)/shard_map/all_to_all | solution.py:185
  214.2 2.1 fusion.66
  218.3 1.0 multiply_bitcast_fusion
  219.4 5.7 %all-to-all-done.2 = bf16[16,4,1,4,1024]{4,1,3,2,0:T(4,128)(2,1)S(1)} async-done(((bf16[16,4,1,4,1024]{4,1,3,2,0:T(4,128)(2,1)}), bf16[16,4,1,4,1024]{4,1,3,2,0:T(4,128)(2,1)S(1)}, u32[]{:S(2)}, u32[]{:S(2)}) %all-to-all-start.2) | async-done | bytes 524320 | tf_op jit(solution)/shard_map/all_to_all | solution.py:185
  225.6 2.4 %fusion.24 = bf16[16,4,1,8,128]{4,3,1,0,2:T(8,128)(2,1)S(1)} fusion(bf16[16,512,1,2,128]{1,4,3,0,2:T(8,128)(2,1)} %bitcast.201, f32[16,4,1,8,512]{4,3,1,0,2:T(8,128)S(1)} %get-tuple-element.13, f32[16,4,8]{2,1,0:T(4,128)S(1)} %get-tuple-element.12, f32[16,4,1,8,128]{4,3,0,1,2:T(8,128)S(1)} %bitcast.209, f32[16]{0:T(128)S(1)} %get-tuple-element.16, ...), kind=kOutput, calls=%fused_computation.30 | convolution fusion | flops 68026368 | bytes 3547200 | tf_op jit(solution)/shard_map/sthgm,smhd->sthgd/dot_general | solution.py:84
  (53 shorter events, 9.9 us)
Async XLA Ops:
  7.2 29.5 %all-gather.5.cloned.1.call-start = ((), (), s32[]{:S(2)}) async-start(), calls=%async_computation.3 | async-start | bytes 1179648 | tf_op jit(solution)/shard_map/all_gather | solution.py:145
  49.6 69.7 %all-to-all-start = ((bf16[16,4,4,8192]{3,2,1,0:T(4,128)(2,1)}), bf16[16,4,4,8192]{3,2,1,0:T(4,128)(2,1)}, u32[]{:S(2)}, u32[]{:S(2)}) async-start(bf16[16,4,4,8192]{3,2,1,0:T(4,128)(2,1)} %reshape.309), calls=%async_computation | async-start | bytes 8388608 | tf_op jit(solution)/shard_map/all_to_all | solution.py:150
  56.3 148.7 %all-gather.7.cloned.1.call-start = ((), (), s32[]{:S(2)}) async-start(), calls=%async_computation.4 | async-start | bytes 4718592 | tf_op jit(solution)/shard_map/all_gather | solution.py:162
  155.4 17.5 %copy-start = (bf16[16,4,1024]{2,1,0:T(4,128)(2,1)S(1)}, bf16[16,4,1024]{2,1,0:T(4,128)(2,1)}, u32[]{:S(2)}) copy-start(bf16[16,4,1024]{2,1,0:T(4,128)(2,1)} %param.6) | copy-start | bytes 393220
  155.4 24.1 %copy-start.1 = (s32[16]{0:T(128)S(1)}, s32[16]{0:T(128)}, u32[]{:S(2)}) copy-start(s32[16]{0:T(128)} %param.11) | copy-start | bytes 196
  196.0 12.1 %all-to-all-start.1 = ((f32[16,1,128]{2,1,0:T(1,128)}), f32[16,1,128]{2,1,0:T(1,128)S(1)}, u32[]{:S(2)}, u32[]{:S(2)}) async-start(f32[16,1,128]{2,1,0:T(1,128)} %reshape.335), calls=%async_computation.1 | async-start | bytes 16384 | tf_op jit(solution)/shard_map/all_to_all | solution.py:186
  208.1 16.9 %all-to-all-start.2 = ((bf16[16,4,1,4,1024]{4,1,3,2,0:T(4,128)(2,1)}), bf16[16,4,1,4,1024]{4,1,3,2,0:T(4,128)(2,1)S(1)}, u32[]{:S(2)}, u32[]{:S(2)}) async-start(bf16[16,4,1,4,1024]{4,1,3,2,0:T(4,128)(2,1)} %copy.154), calls=%async_computation.2 | async-start | bytes 1048576 | tf_op jit(solution)/shard_map/all_to_all | solution.py:185
Sparse Core Ops, SparseCore 0:
  9.7 26.9 all-gather.4
  173.0 31.9 all-gather.6
where the time goes:
time: 237 us; the launch traced here: 236 us
  waiting for transfers between devices  77.6 us (33%)
  local copies, waits for them, and re-layouts  46.8 us (20%)
  matrix products  45 us (19%)
  other arithmetic  19.8 us (8%)
  starting transfers between devices  17.9 us (8%)
  blocking collectives  14.4 us (6%)
  between operations  14.3 us (6%)
    all_to_all x1, waiting for transfers between devices, per_device(): lax.all_to_all(packed, 'prompt', split_axis=0, concat_axis=0, tiled=True)  41.5 us
    unnamed x11, local copies, waits for them, and re-layouts  34.8 us
    all_gather x1, waiting for transfers between devices, per_device(): all_heads = lax.all_gather(probe_vectors, 'ctx', axis=2, tiled=True)  25.5 us
    dot_general x1, matrix products, prefix_attention(): jnp.einsum('hrgn,nhd->hrgd', weights.astype(jnp.bfloat16), shard_rows[:,...  17.5 us
    dot_general x1, matrix products, prefix_attention(): jnp.einsum('rhgd,nhd->hrgn', query_view, shard_rows[:, :, 0], preferred_e...  16.6 us
    all_gather x1, blocking collectives, per_device(): every_lse = lax.all_gather(part_lse[None], 'ctx', axis=0, tiled=True)  14.4 us
    reduce_sum x1, other arithmetic, prefix_attention(): totals = jnp.sum(weights, axis=-1)  14 us
    reshape x1, local copies, waits for them, and re-layouts, per_device(): packed.reshape(row_count, CAP, decode_step_count, QUERY_HEADS * HEAD_SIZE)  7.84 us
  transfers between devices with their start and end apart: 5, of which 4 were waited for; matrix products, arithmetic and copies ran while one was open for 18% of the time, Pallas kernels for 0%

commit v1 on v0

v1 whole, which is shorter than its diff:
```python
import functools

import jax
import jax.numpy as jnp
from jax import lax
from jax.experimental import pallas as pl
from jax.experimental.pallas import tpu as pltpu
from jax.sharding import PartitionSpec as P

QUERY_HEADS = 64
KEY_VALUE_HEADS = 8
HEAD_SIZE = 128
SAMPLE_COUNT = 8
CAP = 4
OWNER_SLOTS = 16
STEPS = 4
GROUP = QUERY_HEADS // KEY_VALUE_HEADS
WIDTH = GROUP * HEAD_SIZE
PAYLOAD = WIDTH + 128
ROWS = SAMPLE_COUNT * STEPS
SLOT_ROWS = OWNER_SLOTS * STEPS
PAIR_ROWS = CAP * STEPS
CHUNK = 1024
LOG2E = 1.4426950408889634
LN2 = 0.6931471805599453
SCALE = HEAD_SIZE**-0.5 * LOG2E
F32 = jnp.float32
BF16 = jnp.bfloat16
MESH = pl.DeviceIdType.MESH


def iota(shape, dim):
    return lax.broadcasted_iota(jnp.int32, shape, dim)


def one_hot(condition):
    return jnp.where(condition, 1.0, 0.0).astype(F32)


def dot(a, b):
    return jnp.dot(a, b, preferred_element_type=F32)


def dot_rows(a, b):
    return lax.dot_general(a, b, (((1,), (1,)), ((), ())), preferred_element_type=F32)


def layout_vectors(active, holder):
    count = holder.shape[1]
    rows, lanes = iota((count, count), 0), iota((count, count), 1)
    diagonal = rows == lanes
    owner_row = holder.astype(F32)
    owner_col = jnp.sum(jnp.where(diagonal, owner_row, 0.0), axis=1, keepdims=True)
    prompts = active.shape[1]
    in_prompt = iota((count, prompts), 0) // SAMPLE_COUNT == iota((count, prompts), 1)
    kept = jnp.sum(jnp.where(in_prompt, active.astype(F32), 0.0), axis=1, keepdims=True)
    live_col = one_hot((iota((count, 1), 0) % SAMPLE_COUNT).astype(F32) < kept)
    live_row = jnp.sum(jnp.where(diagonal, live_col, 0.0), axis=0, keepdims=True)
    same_owner = owner_col == owner_row
    same_prompt = rows // SAMPLE_COUNT == lanes // SAMPLE_COUNT
    before_row = jnp.where(same_owner & (rows < lanes), live_col, 0.0)
    before_col = jnp.where(same_owner & (lanes < rows), live_row, 0.0)
    slot_row = jnp.sum(before_row, axis=0, keepdims=True)
    slot_col = jnp.sum(before_col, axis=1, keepdims=True)
    ordinal_row = jnp.sum(jnp.where(same_prompt, before_row, 0.0), axis=0, keepdims=True)
    ordinal_col = jnp.sum(jnp.where(same_prompt, before_col, 0.0), axis=1, keepdims=True)
    return (owner_row, live_row, slot_row, ordinal_row), (owner_col, live_col, slot_col, ordinal_col)


def same_step(rows, columns):
    return iota((rows, columns), 0) % STEPS == iota((rows, columns), 1) % STEPS


def split_query(block):
    scaled = block.astype(F32) * SCALE
    high = scaled.astype(BF16)
    low = (scaled - high.astype(F32)).astype(BF16)
    pieces = [
        jnp.concatenate(
            [high[:, g * HEAD_SIZE : (g + 1) * HEAD_SIZE], low[:, g * HEAD_SIZE : (g + 1) * HEAD_SIZE]],
            axis=1,
        )
        for g in range(GROUP)
    ]
    return jnp.concatenate(pieces, axis=0)


def twice(keys):
    return jnp.concatenate([keys, keys], axis=1)


def with_ones(values):
    return jnp.concatenate([values, jnp.ones_like(values)], axis=1)


def by_group_lane(column_blocks, rows, copies):
    lane = iota((rows, 128), 1)
    out = jnp.zeros((rows, 128), F32)
    for g in range(GROUP):
        here = (lane % GROUP == g) & (lane < copies * GROUP)
        out = jnp.where(here, column_blocks[g * rows : (g + 1) * rows, :], out)
    return out


def three_terms(value):
    lane = iota(value.shape, 1)
    high = value.astype(BF16).astype(F32)
    rest = value - high
    middle = rest.astype(BF16).astype(F32)
    low = rest - middle
    out = jnp.where(lane < GROUP, high, jnp.where(lane < 2 * GROUP, middle, low))
    return jnp.where(lane < 3 * GROUP, out, 0.0).astype(BF16)


def sum_terms(terms):
    value = terms.astype(F32)
    return value + pltpu.roll(value, 128 - GROUP, 1) + pltpu.roll(value, 128 - 2 * GROUP, 1)


def spread_terms(value):
    lane = iota(value.shape, 1)
    return jnp.where(
        lane < GROUP,
        value,
        jnp.where(lane < 2 * GROUP, pltpu.roll(value, GROUP, 1), pltpu.roll(value, 2 * GROUP, 1)),
    )


def kernel(
    probes,
    active,
    holder,
    fill,
    tail_hbm,
    lead_hbm,
    out_ref,
    mass_ref,
    tail,
    lead,
    send_q,
    recv_q,
    heads_q,
    part_out,
    part_in,
    ret_out,
    ret_in,
    suffix,
    suffix_lse,
    take_table,
    back_table,
    home_table,
    tail_sem,
    lead_sem,
    q_send,
    q_recv,
    c_send,
    c_recv,
    p_send,
    p_recv,
    r_send,
    r_recv,
):
    row_count = lax.axis_size("prompt")
    ctx_count = lax.axis_size("ctx")
    x_count = ctx_count // 2
    me = lax.axis_index("prompt")
    ctx = lax.axis_index("ctx")
    my_x, my_core = ctx // 2, ctx % 2
    span = lead_hbm.shape[0]
    chunk = min(CHUNK, span)
    pairs = row_count * PAIR_ROWS

    def pair_block(index):
        return pl.ds(pl.multiple_of(index * PAIR_ROWS, PAIR_ROWS), PAIR_ROWS)

    def toward(k):
        x = (my_x + (k + 1) // 2) % x_count
        return x * 2 + (my_core + k) % 2

    def away(k):
        x = (my_x + x_count - ((k + 1) // 2) % x_count) % x_count
        return x * 2 + (my_core + k) % 2

    barrier = pltpu.get_barrier_semaphore()

    def greet_prompt(k, _):
        pl.semaphore_signal(
            barrier, inc=1, device_id={"prompt": (me + k) % row_count}, device_id_type=MESH
        )
        return 0

    def greet_ctx(k, _):
        pl.semaphore_signal(barrier, inc=1, device_id={"ctx": (ctx + k) % ctx_count}, device_id_type=MESH)
        return 0

    lax.fori_loop(1, row_count, greet_prompt, 0)
    lax.fori_loop(1, ctx_count, greet_ctx, 0)

    tail_copy = pltpu.make_async_copy(tail_hbm, tail, tail_sem)
    tail_copy.start()

    def lead_copy(k):
        head = toward(k)
        return pltpu.make_async_copy(
            lead_hbm.at[:, pl.ds(pl.multiple_of(head * 2 * HEAD_SIZE, 2 * HEAD_SIZE), 2 * HEAD_SIZE)],
            lead.at[k],
            lead_sem.at[k],
        )

    def start_lead(k, _):
        lead_copy(k).start()
        return 0

    lax.fori_loop(0, ctx_count, start_lead, 0)

    row_form, col_form = layout_vectors(active[...], holder[...])
    owner_row, live_row, slot_row, ordinal_row = row_form
    owner_col, live_col, slot_col, ordinal_col = col_form
    count = owner_row.shape[1]
    my_row = me.astype(F32)

    pair_of_row = iota((pairs, count), 0) // STEPS
    pair_of_col = iota((count, pairs), 1) // STEPS
    sample_of_lane = iota((pairs, count), 1)
    sample_of_row = iota((count, pairs), 0)
    mine_row = live_row * one_hot(owner_row == my_row)
    to_pair = jnp.where(
        (pair_of_row // CAP == sample_of_lane // SAMPLE_COUNT)
        & ((pair_of_row % CAP).astype(F32) == ordinal_row),
        mine_row,
        0.0,
    )
    from_slot = one_hot((iota((count, SLOT_ROWS), 1) // STEPS).astype(F32) == slot_col)
    send_table = jnp.where(
        same_step(pairs, SLOT_ROWS), dot(to_pair.astype(BF16), from_slot.astype(BF16)), 0.0
    ).astype(BF16)
    packed = dot(send_table, probes[...]).astype(BF16)
    send_q[...] = packed

    pl.semaphore_wait(barrier, row_count - 1 + ctx_count - 1)

    def q_copy(k):
        peer = (me + k) % row_count
        return pltpu.make_async_remote_copy(
            src_ref=send_q.at[pair_block(peer)],
            dst_ref=recv_q.at[pair_block(me)],
            send_sem=q_send.at[k],
            recv_sem=q_recv.at[k],
            device_id={"prompt": peer},
            device_id_type=MESH,
        )

    def start_q(k, _):
        q_copy(k).start()
        return 0

    lax.fori_loop(1, row_count, start_q, 0)
    recv_q[pair_block(me), :] = send_q[pair_block(me), :]

    as_sample = jnp.where(
        (iota((ROWS, count), 1) // SAMPLE_COUNT == me)
        & (iota((ROWS, count), 1) % SAMPLE_COUNT == iota((ROWS, count), 0) // STEPS),
        live_row,
        0.0,
    )
    at_pair = one_hot(
        ((pair_of_col // CAP).astype(F32) == owner_col) & ((pair_of_col % CAP).astype(F32) == ordinal_col)
    )
    take_table[...] = jnp.where(
        same_step(ROWS, pairs), dot(as_sample.astype(BF16), at_pair.astype(BF16)), 0.0
    ).astype(BF16)
    of_pair = one_hot(
        ((pair_of_row // CAP).astype(F32) == owner_row) & ((pair_of_row % CAP).astype(F32) == ordinal_row)
    )
    of_sample = jnp.where(
        (iota((count, ROWS), 0) // SAMPLE_COUNT == me)
        & (iota((count, ROWS), 0) % SAMPLE_COUNT == iota((count, ROWS), 1) // STEPS),
        live_col,
        0.0,
    )
    back_table[...] = jnp.where(
        same_step(pairs, ROWS), dot(of_pair.astype(BF16), of_sample.astype(BF16)), 0.0
    ).astype(BF16)
    mine_col = live_col * one_hot(owner_col == my_row)
    into_slot = one_hot((iota((SLOT_ROWS, count), 0) // STEPS).astype(F32) == slot_row)
    from_pair = jnp.where(
        (pair_of_col // CAP == sample_of_row // SAMPLE_COUNT)
        & ((pair_of_col % CAP).astype(F32) == ordinal_col),
        mine_col,
        0.0,
    )
    home_table[...] = jnp.where(
        same_step(SLOT_ROWS, pairs), dot(into_slot.astype(BF16), from_pair.astype(BF16)), 0.0
    ).astype(BF16)

    tail_copy.wait()
    batch = 4
    block_rows = batch * STEPS
    tail_rows = GROUP * block_rows
    tail_span = tail.shape[1]

    def suffix_group(q, _):
        rows = pl.ds(pl.multiple_of(q * block_rows, block_rows), block_rows)
        query = split_query(probes[rows, :])
        row = iota((tail_rows, 1), 0)
        which = (row // STEPS) % batch
        scores = jnp.zeros((tail_rows, tail_span), F32)
        for s in range(batch):
            found = dot_rows(query, twice(tail[q * batch + s, :, 0:HEAD_SIZE]))
            scores = jnp.where(which == s, found, scores)
        filled = jnp.sum(
            jnp.where(
                iota((tail_rows, OWNER_SLOTS), 1) == q * batch + which, fill[...].astype(F32), 0.0
            ),
            axis=1,
            keepdims=True,
        )
        limit = filled - (STEPS - 1) + (row % STEPS).astype(F32)
        visible = iota((tail_rows, tail_span), 1).astype(F32) < limit
        scores = jnp.where(visible, scores, -1e30)
        highest = jnp.max(scores, axis=1, keepdims=True)
        weights = jnp.exp2(scores - highest).astype(BF16)
        total = jnp.zeros((tail_rows, 2 * HEAD_SIZE), F32)
        for s in range(batch):
            found = dot(weights, with_ones(tail[q * batch + s, :, HEAD_SIZE:]))
            total = jnp.where(which == s, found, total)
        sums = total[:, HEAD_SIZE:]
        values = total[:, :HEAD_SIZE] / sums
        for g in range(GROUP):
            suffix[rows, g * HEAD_SIZE : (g + 1) * HEAD_SIZE] = values[
                g * block_rows : (g + 1) * block_rows, :
            ]
        suffix_lse[rows, :] = by_group_lane(highest + jnp.log2(sums), block_rows, 1)
        return 0

    lax.fori_loop(0, OWNER_SLOTS // batch, suffix_group, 0)

    def wait_q(k, _):
        q_copy(k).wait_recv()
        return 0

    lax.fori_loop(1, row_count, wait_q, 0)
    heads_q[ctx] = dot(take_table[...], recv_q[...]).astype(BF16)

    def c_copy(k):
        return pltpu.make_async_remote_copy(
            src_ref=heads_q.at[ctx],
            dst_ref=heads_q.at[ctx],
            send_sem=c_send.at[k],
            recv_sem=c_recv.at[k],
            device_id={"ctx": away(k)},
            device_id_type=MESH,
        )

    def start_c(k, _):
        c_copy(k).start()
        return 0

    lax.fori_loop(1, ctx_count, start_c, 0)

    def p_copy(k):
        return pltpu.make_async_remote_copy(
            src_ref=part_out.at[k],
            dst_ref=part_in.at[ctx],
            send_sem=p_send.at[k],
            recv_sem=p_recv.at[k],
            device_id={"ctx": toward(k)},
            device_id_type=MESH,
        )

    def prefix_head(k):
        lead_copy(k).wait()
        query = split_query(heads_q[toward(k)])
        rows = query.shape[0]

        def scores_of(i):
            return dot_rows(query, twice(lead[k, i * chunk : (i + 1) * chunk, 0:HEAD_SIZE]))

        highest = jnp.full((rows, 1), -1e30, F32)
        total = jnp.zeros((rows, 2 * HEAD_SIZE), F32)
        scores = scores_of(0)
        for i in range(span // chunk):
            later = scores_of(i + 1) if (i + 1) * chunk < span else None
            top = jnp.maximum(highest, jnp.max(scores, axis=1, keepdims=True))
            weights = jnp.exp2(scores - top).astype(BF16)
            total = total * jnp.exp2(highest - top) + dot(
                weights, with_ones(lead[k, i * chunk : (i + 1) * chunk, HEAD_SIZE:])
            )
            highest, scores = top, later
        sums = total[:, HEAD_SIZE:]
        values = (total[:, :HEAD_SIZE] / sums).astype(BF16)
        for g in range(GROUP):
            part_out[k, :, g * HEAD_SIZE : (g + 1) * HEAD_SIZE] = values[g * ROWS : (g + 1) * ROWS, :]
        part_out[k, :, WIDTH:] = three_terms(by_group_lane(highest + jnp.log2(sums), ROWS, 3))

    prefix_head(0)
    part_in[ctx] = part_out[0]

    def prefix_step(k, _):
        c_copy(k).wait_recv()
        prefix_head(k)
        p_copy(k).start()
        return 0

    lax.fori_loop(1, ctx_count, prefix_step, 0)

    def wait_p(k, _):
        p_copy(k).wait_recv()
        return 0

    lax.fori_loop(1, ctx_count, wait_p, 0)

    masses = [sum_terms(part_in[c, :, WIDTH:]) for c in range(ctx_count)]
    highest = functools.reduce(jnp.maximum, masses)
    shares = [jnp.exp2(mass - highest) for mass in masses]
    whole = functools.reduce(jnp.add, shares)
    shares = [share / whole for share in shares]
    merged = []
    for g in range(GROUP):
        columns = slice(g * HEAD_SIZE, (g + 1) * HEAD_SIZE)
        acc = jnp.zeros((ROWS, HEAD_SIZE), F32)
        for c in range(ctx_count):
            acc = acc + shares[c][:, g : g + 1] * part_in[c, :, columns].astype(F32)
        merged.append(acc.astype(BF16))
    merged.append(three_terms(spread_terms(highest + jnp.log2(whole))))
    ret_out[...] = dot(back_table[...], jnp.concatenate(merged, axis=1)).astype(BF16)

    def r_copy(k):
        peer = (me + k) % row_count
        return pltpu.make_async_remote_copy(
            src_ref=ret_out.at[pair_block(peer)],
            dst_ref=ret_in.at[pair_block(me)],
            send_sem=r_send.at[k],
            recv_sem=r_recv.at[k],
            device_id={"prompt": peer},
            device_id_type=MESH,
        )

    def start_r(k, _):
        r_copy(k).start()
        return 0

    lax.fori_loop(1, row_count, start_r, 0)
    ret_in[pair_block(me), :] = ret_out[pair_block(me), :]

    def wait_sends(k, _):
        q_copy(k).wait_send()
        return 0

    lax.fori_loop(1, row_count, wait_sends, 0)

    def wait_ctx_sends(k, _):
        c_copy(k).wait_send()
        p_copy(k).wait_send()
        return 0

    lax.fori_loop(1, ctx_count, wait_ctx_sends, 0)

    def wait_r(k, _):
        r_copy(k).wait_recv()
        return 0

    lax.fori_loop(1, row_count, wait_r, 0)

    home = dot(home_table[...], ret_in[...])
    alive = jnp.sum(home_table[...].astype(F32), axis=1, keepdims=True)
    prefix_mass = sum_terms(home[:, WIDTH:])
    suffix_mass = suffix_lse[...]
    top = jnp.maximum(prefix_mass, suffix_mass)
    mass = top + jnp.log2(jnp.exp2(prefix_mass - top) + jnp.exp2(suffix_mass - top))
    prefix_share = jnp.exp2(prefix_mass - mass) * alive
    suffix_share = jnp.exp2(suffix_mass - mass) * alive
    for g in range(GROUP):
        columns = slice(g * HEAD_SIZE, (g + 1) * HEAD_SIZE)
        out_ref[:, columns] = (
            prefix_share[:, g : g + 1] * home[:, columns] + suffix_share[:, g : g + 1] * suffix[:, columns]
        ).astype(BF16)
    mass_ref[...] = (mass * (alive * LN2))[:, :GROUP]

    def wait_r_sends(k, _):
        r_copy(k).wait_send()
        return 0

    lax.fori_loop(1, row_count, wait_r_sends, 0)


def per_device(probe_vectors, tail_memory, lead_memory, active_rollouts, holder_map, tail_fill):
    row_count = lax.axis_size("prompt")
    ctx_count = lax.axis_size("ctx")
    slots, steps, width = probe_vectors.shape
    span = lead_memory.shape[1]
    tail_span = tail_memory.shape[1]
    pairs = row_count * PAIR_ROWS
    vmem = pl.BlockSpec(memory_space=pltpu.VMEM)
    anywhere = pl.BlockSpec(memory_space=pl.ANY)
    dma = pltpu.SemaphoreType.DMA
    attended, log_mass = pl.pallas_call(
        kernel,
        out_shape=(
            jax.ShapeDtypeStruct((slots * steps, width), BF16),
            jax.ShapeDtypeStruct((slots * steps, GROUP), F32),
        ),
        in_specs=[vmem, vmem, vmem, vmem, anywhere, anywhere],
        out_specs=(vmem, vmem),
        scratch_shapes=[
            pltpu.VMEM((slots, tail_span, 2 * HEAD_SIZE), BF16),
            pltpu.VMEM((ctx_count, span, 2 * HEAD_SIZE), BF16),
            pltpu.VMEM((pairs, WIDTH), BF16),
            pltpu.VMEM((pairs, WIDTH), BF16),
            pltpu.VMEM((ctx_count, ROWS, WIDTH), BF16),
            pltpu.VMEM((ctx_count, ROWS, PAYLOAD), BF16),
            pltpu.VMEM((ctx_count, ROWS, PAYLOAD), BF16),
            pltpu.VMEM((pairs, PAYLOAD), BF16),
            pltpu.VMEM((pairs, PAYLOAD), BF16),
            pltpu.VMEM((SLOT_ROWS, WIDTH), F32),
            pltpu.VMEM((SLOT_ROWS, 128), F32),
            pltpu.VMEM((ROWS, pairs), BF16),
            pltpu.VMEM((pairs, ROWS), BF16),
            pltpu.VMEM((SLOT_ROWS, pairs), BF16),
            dma,
            dma((ctx_count,)),
            dma((row_count,)),
            dma((row_count,)),
            dma((ctx_count,)),
            dma((ctx_count,)),
            dma((ctx_count,)),
            dma((ctx_count,)),
            dma((row_count,)),
            dma((row_count,)),
        ],
        compiler_params=pltpu.CompilerParams(
            collective_id=0, has_side_effects=True, vmem_limit_bytes=56 * 2**20
        ),
        cost_estimate=pl.CostEstimate(
            flops=5_000_000_000, bytes_accessed=22_000_000, transcendentals=9_000_000
        ),
        name="grouped_attention",
    )(
        probe_vectors.reshape(slots * steps, width),
        active_rollouts.reshape(1, -1),
        holder_map.reshape(1, -1),
        tail_fill.reshape(1, -1),
        tail_memory,
        lead_memory.reshape(span, -1),
    )
    return attended.reshape(slots, steps, width), log_mass.reshape(slots, steps, GROUP)


def solution(mesh):
    return jax.shard_map(
        per_device,
        mesh=mesh,
        in_specs=(
            P("prompt", None, "ctx"),
            P("prompt", None, "ctx"),
            P("prompt", "ctx", None),
            P(),
            P(),
            P("prompt"),
        ),
        out_specs=(P("prompt", None, "ctx"), P("prompt", None, "ctx")),
        check_vma=False,
    )
```

time: 237 us -> 52.5 us (0.22)
  the two profiles are of different devices: /device:TPU:1 before, /device:TPU:2 now
where the time goes in v1:
time: 52.5 us; the launch traced here: 52.3 us
  Pallas kernels  47 us (90%)
  local copies, waits for them, and re-layouts  4.64 us (9%)
  between operations  0.64 us (1%)
    pallas_call x1, Pallas kernels, per_device(): pl.pallas_call(kernel, out_shape=(jax.ShapeDtypeStruct((slots * steps, wi...  47 us
    reshape x1, local copies, waits for them, and re-layouts, per_device(): attended.reshape(slots, steps, width)  1.62 us
    reshape x1, local copies, waits for them, and re-layouts, per_device(): probe_vectors.reshape(slots * steps, width)  1.59 us
    unnamed x1, local copies, waits for them, and re-layouts  1.43 us

profile of v1, /device:TPU:2, one launch (start us, length us, event | category | flops | bytes accessed | tf_op | source)
XLA Modules:
  0.0 52.3 jit_solution(12535619403143474234)
XLA Ops:
  0.6 1.6 %reshape.25.probes = bf16[64,1024]{1,0:T(8,128)(2,1)} reshape(bf16[16,4,1024]{2,1,0:T(4,128)(2,1)} %param.6) | data formatting | bytes 262144 | tf_op jit(solution)/shard_map/reshape | solution.py:539
  2.2 47.0 %grouped_attention.1 = (bf16[64,1024]{1,0:T(8,128)(2,1)}, f32[64,8]{1,0:T(8,128)}) custom-call(bf16[64,1024]{1,0:T(8,128)(2,1)} %reshape.25.probes, s32[1,16]{1,0:T(1,128)} %bitcast.7, s32[1,128]{1,0:T(1,128)} %bitcast.8, s32[1,16]{1,0:T(1,128)} %bitcast.9, bf16[16,512,256]{2,1,0:T(8,128)(2,1)} %tail_hbm.1, bf16[4096,2048]{1,0:T(8,128)(2,1)} %bitcast.5), custom_call_target="tpu_custom_call" | custom-call | flops 5000000000 | bytes 22000000 | tf_op jit(solution)/shard_map/grouped_attention/pallas_call | solution.py:497
  49.3 1.6 %reshape.30 = bf16[16,4,1024]{2,1,0:T(4,128)(2,1)} reshape(bf16[64,1024]{1,0:T(8,128)(2,1)} %get-tuple-element.4) | data formatting | bytes 262144 | tf_op jit(solution)/shard_map/reshape | solution.py:546
  50.9 1.4 %copy.8 = f32[16,4,8]{0,2,1:T(8,128)} copy(f32[16,4,8]{2,1,0:T(4,128)} %bitcast.6) | data formatting | bytes 4096

commit v2 on v1

--- a/solution.py
+++ b/solution.py
@@ -21,6 +21,9 @@
 SLOT_ROWS = OWNER_SLOTS * STEPS
 PAIR_ROWS = CAP * STEPS
 CHUNK = 1024
+EARLY_GROUPS = 4
+LATE_GROUPS = 0
+FINISH_STEP = 6
 LOG2E = 1.4426950408889634
 LN2 = 0.6931471805599453
 SCALE = HEAD_SIZE**-0.5 * LOG2E
@@ -127,21 +130,28 @@
 
 
 def kernel(
+    probes_hbm,
+    active_hbm,
+    holder_hbm,
+    fill_hbm,
+    tail_hbm,
+    lead_hbm,
+    out_ref,
+    mass_ref,
     probes,
     active,
     holder,
     fill,
-    tail_hbm,
-    lead_hbm,
-    out_ref,
-    mass_ref,
     tail,
     lead,
+    queries,
     send_q,
     recv_q,
     heads_q,
     part_out,
-    part_in,
+    twin_in,
+    pair_out,
+    pair_in,
     ret_out,
     ret_in,
     suffix,
@@ -149,12 +159,15 @@
     take_table,
     back_table,
     home_table,
+    small_sem,
     tail_sem,
     lead_sem,
     q_send,
     q_recv,
     c_send,
     c_recv,
+    t_send,
+    t_recv,
     p_send,
     p_recv,
     r_send,
@@ -163,55 +176,78 @@
     row_count = lax.axis_size("prompt")
     ctx_count = lax.axis_size("ctx")
     x_count = ctx_count // 2
+    y_count = min(4, row_count)
+    z_count = row_count // y_count
     me = lax.axis_index("prompt")
     ctx = lax.axis_index("ctx")
-    my_x, my_core = ctx // 2, ctx % 2
+    x, core = ctx // 2, ctx % 2
+    z, y = me // y_count, me % y_count
     span = lead_hbm.shape[0]
     chunk = min(CHUNK, span)
     pairs = row_count * PAIR_ROWS
 
+    def ring(a, size):
+        return min(a, size - a)
+
+    row_offsets = sorted(
+        [(a, b) for a in range(z_count) for b in range(y_count) if a or b],
+        key=lambda ab: -ring(ab[0], z_count) - ring(ab[1], y_count),
+    )
+    ctx_offsets = sorted(
+        [(a, b) for a in range(x_count) for b in range(2) if a or b],
+        key=lambda ab: -2 * ring(ab[0], x_count) - ab[1],
+    )
+
+    def row_peer(offset):
+        return ((z + offset[0]) % z_count) * y_count + (y + offset[1]) % y_count
+
+    def ctx_peer(offset):
+        return ((x + offset[0]) % x_count) * 2 + (core + offset[1]) % 2
+
     def pair_block(index):
         return pl.ds(pl.multiple_of(index * PAIR_ROWS, PAIR_ROWS), PAIR_ROWS)
 
-    def toward(k):
-        x = (my_x + (k + 1) // 2) % x_count
-        return x * 2 + (my_core + k) % 2
-
-    def away(k):
-        x = (my_x + x_count - ((k + 1) // 2) % x_count) % x_count
-        return x * 2 + (my_core + k) % 2
-
     barrier = pltpu.get_barrier_semaphore()
-
-    def greet_prompt(k, _):
-        pl.semaphore_signal(
-            barrier, inc=1, device_id={"prompt": (me + k) % row_count}, device_id_type=MESH
-        )
-        return 0
-
-    def greet_ctx(k, _):
-        pl.semaphore_signal(barrier, inc=1, device_id={"ctx": (ctx + k) % ctx_count}, device_id_type=MESH)
-        return 0
-
-    lax.fori_loop(1, row_count, greet_prompt, 0)
-    lax.fori_loop(1, ctx_count, greet_ctx, 0)
+    for offset in row_offsets:
+        pl.semaphore_signal(barrier, inc=1, device_id={"prompt": row_peer(offset)}, device_id_type=MESH)
+    for offset in ctx_offsets:
+        pl.semaphore_signal(barrier, inc=1, device_id={"ctx": ctx_peer(offset)}, device_id_type=MESH)
+
+    small_copies = [
+        pltpu.make_async_copy(source, target, small_sem.at[i])
+        for i, (source, target) in enumerate(
+            [(active_hbm, active), (holder_hbm, holder), (probes_hbm, probes), (fill_hbm, fill)]
+        )
+    ]
+    for copy in small_copies:
+        copy.start()
+
+    def step_x(s):
+        return (x + s % x_count + s // x_count) % x_count
+
+    def step_core(s):
+        return s // x_count
+
+    def step_head(s):
+        return step_x(s) * 2 + step_core(s)
 
     tail_copy = pltpu.make_async_copy(tail_hbm, tail, tail_sem)
     tail_copy.start()
 
-    def lead_copy(k):
-        head = toward(k)
+    def lead_copy(s):
+        first = pl.multiple_of(step_head(s) * 2 * HEAD_SIZE, 2 * HEAD_SIZE)
         return pltpu.make_async_copy(
-            lead_hbm.at[:, pl.ds(pl.multiple_of(head * 2 * HEAD_SIZE, 2 * HEAD_SIZE), 2 * HEAD_SIZE)],
-            lead.at[k],
-            lead_sem.at[k],
-        )
-
-    def start_lead(k, _):
-        lead_copy(k).start()
+            lead_hbm.at[:, pl.ds(first, 2 * HEAD_SIZE)], lead.at[s], lead_sem.at[s]
+        )
+
+    def start_lead(s, _):
+        lead_copy(s).start()
         return 0
 
     lax.fori_loop(0, ctx_count, start_lead, 0)
+
+    for copy in small_copies:
+        copy.wait()
 
     row_form, col_form = layout_vectors(active[...], holder[...])
     owner_row, live_row, slot_row, ordinal_row = row_form
@@ -234,27 +270,27 @@
     send_table = jnp.where(
         same_step(pairs, SLOT_ROWS), dot(to_pair.astype(BF16), from_slot.astype(BF16)), 0.0
     ).astype(BF16)
-    packed = dot(send_table, probes[...]).astype(BF16)
-    send_q[...] = packed
+    queries[...] = probes[...].astype(F32).reshape(SLOT_ROWS, WIDTH).astype(BF16)
+    send_q[...] = dot(send_table, queries[...]).astype(BF16)
 
     pl.semaphore_wait(barrier, row_count - 1 + ctx_count - 1)
 
-    def q_copy(k):
-        peer = (me + k) % row_count
+    def q_copy(i):
+        peer = row_peer(row_offsets[i])
         return pltpu.make_async_remote_copy(
             src_ref=send_q.at[pair_block(peer)],
             dst_ref=recv_q.at[pair_block(me)],
-            send_sem=q_send.at[k],
-            recv_sem=q_recv.at[k],
+            send_sem=q_send.at[i],
+            recv_sem=q_recv.at[i],
             device_id={"prompt": peer},
             device_id_type=MESH,
         )
 
-    def start_q(k, _):
-        q_copy(k).start()
-        return 0
-
-    lax.fori_loop(1, row_count, start_q, 0)
+    def start_q():
+        for i in range(row_count - 1):
+            q_copy(i).start()
+
+    pl.when(core == 0)(start_q)
     recv_q[pair_block(me), :] = send_q[pair_block(me), :]
 
     as_sample = jnp.where(
@@ -301,7 +337,7 @@
 
     def suffix_group(q, _):
         rows = pl.ds(pl.multiple_of(q * block_rows, block_rows), block_rows)
-        query = split_query(probes[rows, :])
+        query = split_query(queries[rows, :])
         row = iota((tail_rows, 1), 0)
         which = (row // STEPS) % batch
         scores = jnp.zeros((tail_rows, tail_span), F32)
@@ -333,48 +369,130 @@
         suffix_lse[rows, :] = by_group_lane(highest + jnp.log2(sums), block_rows, 1)
         return 0
 
-    lax.fori_loop(0, OWNER_SLOTS // batch, suffix_group, 0)
-
-    def wait_q(k, _):
-        q_copy(k).wait_recv()
-        return 0
-
-    lax.fori_loop(1, row_count, wait_q, 0)
-    heads_q[ctx] = dot(take_table[...], recv_q[...]).astype(BF16)
-
-    def c_copy(k):
+    groups = OWNER_SLOTS // batch
+    lax.fori_loop(0, EARLY_GROUPS, suffix_group, 0)
+    pl.when(core == 1)(start_q)
+    lax.fori_loop(EARLY_GROUPS, groups - LATE_GROUPS, suffix_group, 0)
+
+    def c_copy(i):
         return pltpu.make_async_remote_copy(
             src_ref=heads_q.at[ctx],
             dst_ref=heads_q.at[ctx],
-            send_sem=c_send.at[k],
-            recv_sem=c_recv.at[k],
-            device_id={"ctx": away(k)},
+            send_sem=c_send.at[i],
+            recv_sem=c_recv.at[ctx],
+            device_id={"ctx": ctx_peer(ctx_offsets[i])},
             device_id_type=MESH,
         )
 
-    def start_c(k, _):
-        c_copy(k).start()
-        return 0
-
-    lax.fori_loop(1, ctx_count, start_c, 0)
-
-    def p_copy(k):
+    def c_arrival(head):
         return pltpu.make_async_remote_copy(
-            src_ref=part_out.at[k],
-            dst_ref=part_in.at[ctx],
-            send_sem=p_send.at[k],
-            recv_sem=p_recv.at[k],
-            device_id={"ctx": toward(k)},
+            src_ref=heads_q.at[head],
+            dst_ref=heads_q.at[head],
+            send_sem=c_send.at[0],
+            recv_sem=c_recv.at[head],
+            device_id={"ctx": ctx_peer((0, 1))},
             device_id_type=MESH,
         )
 
-    def prefix_head(k):
-        lead_copy(k).wait()
-        query = split_query(heads_q[toward(k)])
+    def take_queries():
+        for i in range(row_count - 1):
+            q_copy(i).wait_recv()
+        heads_q[ctx] = dot(take_table[...], recv_q[...]).astype(BF16)
+        for i in reversed(range(ctx_count - 1)):
+            c_copy(i).start()
+
+    def t_copy(j):
+        return pltpu.make_async_remote_copy(
+            src_ref=part_out.at[(1 - core) * x_count + j],
+            dst_ref=twin_in.at[j],
+            send_sem=t_send.at[j],
+            recv_sem=t_recv.at[j],
+            device_id={"ctx": ctx_peer((0, 1))},
+            device_id_type=MESH,
+        )
+
+    def p_copy(j):
+        return pltpu.make_async_remote_copy(
+            src_ref=pair_out.at[j],
+            dst_ref=pair_in.at[x],
+            send_sem=p_send.at[j],
+            recv_sem=p_recv.at[x],
+            device_id={"ctx": step_x(core * x_count + j) * 2 + core},
+            device_id_type=MESH,
+        )
+
+    def p_arrival(offset):
+        source = (x + offset) % x_count
+        return pltpu.make_async_remote_copy(
+            src_ref=pair_out.at[0],
+            dst_ref=pair_in.at[source],
+            send_sem=p_send.at[0],
+            recv_sem=p_recv.at[source],
+            device_id={"ctx": source * 2 + core},
+            device_id_type=MESH,
+        )
+
+    def merge(blocks):
+        masses = [sum_terms(block[:, WIDTH:]) for block in blocks]
+        highest = functools.reduce(jnp.maximum, masses)
+        shares = [jnp.exp2(mass - highest) for mass in masses]
+        whole = functools.reduce(jnp.add, shares)
+        shares = [share / whole for share in shares]
+        merged = []
+        for g in range(GROUP):
+            columns = slice(g * HEAD_SIZE, (g + 1) * HEAD_SIZE)
+            merged.append(
+                functools.reduce(
+                    jnp.add,
+                    [
+                        share[:, g : g + 1] * block[:, columns].astype(F32)
+                        for share, block in zip(shares, blocks)
+                    ],
+                ).astype(BF16)
+            )
+        merged.append(three_terms(spread_terms(highest + jnp.log2(whole))))
+        return jnp.concatenate(merged, axis=1)
+
+    def merge_pair(s):
+        j = s % x_count
+        t_copy(j).wait_recv()
+        both = merge([part_out[s], twin_in[j]])
+
+        @pl.when(step_x(s) == x)
+        def _():
+            pair_in[x] = both
+
+        @pl.when(step_x(s) != x)
+        def _():
+            pair_out[j] = both
+            p_copy(j).start()
+
+    def r_copy(i):
+        peer = row_peer(row_offsets[i])
+        return pltpu.make_async_remote_copy(
+            src_ref=ret_out.at[pair_block(peer)],
+            dst_ref=ret_in.at[pair_block(me)],
+            send_sem=r_send.at[i],
+            recv_sem=r_recv.at[i],
+            device_id={"prompt": peer},
+            device_id_type=MESH,
+        )
+
+    def finish_head():
+        for offset in range(1, x_count):
+            p_arrival(offset).wait_recv()
+        merged = merge([pair_in[i] for i in range(x_count)])
+        ret_out[...] = dot(back_table[...], merged).astype(BF16)
+        for i in range(row_count - 1):
+            r_copy(i).start()
+        ret_in[pair_block(me), :] = ret_out[pair_block(me), :]
+
+    def prefix_head(s):
+        query = split_query(heads_q[step_head(s)])
         rows = query.shape[0]
 
         def scores_of(i):
-            return dot_rows(query, twice(lead[k, i * chunk : (i + 1) * chunk, 0:HEAD_SIZE]))
+            return dot_rows(query, twice(lead[s, i * chunk : (i + 1) * chunk, 0:HEAD_SIZE]))
 
         highest = jnp.full((rows, 1), -1e30, F32)
         total = jnp.zeros((rows, 2 * HEAD_SIZE), F32)
@@ -384,83 +502,60 @@
             top = jnp.maximum(highest, jnp.max(scores, axis=1, keepdims=True))
             weights = jnp.exp2(scores - top).astype(BF16)
             total = total * jnp.exp2(highest - top) + dot(
-                weights, with_ones(lead[k, i * chunk : (i + 1) * chunk, HEAD_SIZE:])
+                weights, with_ones(lead[s, i * chunk : (i + 1) * chunk, HEAD_SIZE:])
             )
             highest, scores = top, later
         sums = total[:, HEAD_SIZE:]
         values = (total[:, :HEAD_SIZE] / sums).astype(BF16)
         for g in range(GROUP):
-            part_out[k, :, g * HEAD_SIZE : (g + 1) * HEAD_SIZE] = values[g * ROWS : (g + 1) * ROWS, :]
-        part_out[k, :, WIDTH:] = three_terms(by_group_lane(highest + jnp.log2(sums), ROWS, 3))
-
-    prefix_head(0)
-    part_in[ctx] = part_out[0]
-
-    def prefix_step(k, _):
-        c_copy(k).wait_recv()
-        prefix_head(k)
-        p_copy(k).start()
+            part_out[s, :, g * HEAD_SIZE : (g + 1) * HEAD_SIZE] = values[g * ROWS : (g + 1) * ROWS, :]
+        part_out[s, :, WIDTH:] = three_terms(by_group_lane(highest + jnp.log2(sums), ROWS, 3))
+
+    def prefix_step(s, _):
+        pl.when(s == core)(take_queries)
+        lead_copy(s).wait()
+
+        @pl.when(step_head(s) != ctx)
+        def _():
+            c_arrival(step_head(s)).wait_recv()
+
+        prefix_head(s)
+        j = s % x_count
+
+        @pl.when(step_core(s) != core)
+        def _():
+            t_copy(j).start()
+
+        merged_step = s - 1 + core
+
+        @pl.when((merged_step >= core * x_count) & (merged_step < (core + 1) * x_count))
+        def _():
+            merge_pair(merged_step)
+
+        if LATE_GROUPS:
+
+            @pl.when(s == 0)
+            def _():
+                lax.fori_loop(groups - LATE_GROUPS, groups, suffix_group, 0)
+
+        pl.when(s == FINISH_STEP + (ctx_count - 1 - FINISH_STEP) * core)(finish_head)
         return 0
 
-    lax.fori_loop(1, ctx_count, prefix_step, 0)
-
-    def wait_p(k, _):
-        p_copy(k).wait_recv()
-        return 0
-
-    lax.fori_loop(1, ctx_count, wait_p, 0)
-
-    masses = [sum_terms(part_in[c, :, WIDTH:]) for c in range(ctx_count)]
-    highest = functools.reduce(jnp.maximum, masses)
-    shares = [jnp.exp2(mass - highest) for mass in masses]
-    whole = functools.reduce(jnp.add, shares)
-    shares = [share / whole for share in shares]
-    merged = []
-    for g in range(GROUP):
-        columns = slice(g * HEAD_SIZE, (g + 1) * HEAD_SIZE)
-        acc = jnp.zeros((ROWS, HEAD_SIZE), F32)
-        for c in range(ctx_count):
-            acc = acc + shares[c][:, g : g + 1] * part_in[c, :, columns].astype(F32)
-        merged.append(acc.astype(BF16))
-    merged.append(three_terms(spread_terms(highest + jnp.log2(whole))))
-    ret_out[...] = dot(back_table[...], jnp.concatenate(merged, axis=1)).astype(BF16)
-
-    def r_copy(k):
-        peer = (me + k) % row_count
-        return pltpu.make_async_remote_copy(
-            src_ref=ret_out.at[pair_block(peer)],
-            dst_ref=ret_in.at[pair_block(me)],
-            send_sem=r_send.at[k],
-            recv_sem=r_recv.at[k],
-            device_id={"prompt": peer},
-            device_id_type=MESH,
-        )
-
-    def start_r(k, _):
-        r_copy(k).start()
-        return 0
-
-    lax.fori_loop(1, row_count, start_r, 0)
-    ret_in[pair_block(me), :] = ret_out[pair_block(me), :]
-
-    def wait_sends(k, _):
-        q_copy(k).wait_send()
-        return 0
-
-    lax.fori_loop(1, row_count, wait_sends, 0)
-
-    def wait_ctx_sends(k, _):
-        c_copy(k).wait_send()
-        p_copy(k).wait_send()
-        return 0
-
-    lax.fori_loop(1, ctx_count, wait_ctx_sends, 0)
-
-    def wait_r(k, _):
-        r_copy(k).wait_recv()
-        return 0
-
-    lax.fori_loop(1, row_count, wait_r, 0)
+    lax.fori_loop(0, ctx_count, prefix_step, 0)
+
+    for i in range(row_count - 1):
+        q_copy(i).wait_send()
+    for i in range(ctx_count - 1):
+        c_copy(i).wait_send()
+    for j in range(x_count):
+        t_copy(j).wait_send()
+
+        @pl.when(step_x(core * x_count + j) != x)
+        def _():
+            p_copy(j).wait_send()
+
+    for i in range(row_count - 1):
+        r_copy(i).wait_recv()
 
     home = dot(home_table[...], ret_in[...])
     alive = jnp.sum(home_table[...].astype(F32), axis=1, keepdims=True)
@@ -472,21 +567,33 @@
     suffix_share = jnp.exp2(suffix_mass - mass) * alive
     for g in range(GROUP):
         columns = slice(g * HEAD_SIZE, (g + 1) * HEAD_SIZE)
-        out_ref[:, columns] = (
+        mixed = (
             prefix_share[:, g : g + 1] * home[:, columns] + suffix_share[:, g : g + 1] * suffix[:, columns]
-        ).astype(BF16)
-    mass_ref[...] = (mass * (alive * LN2))[:, :GROUP]
-
-    def wait_r_sends(k, _):
-        r_copy(k).wait_send()
-        return 0
-
-    lax.fori_loop(1, row_count, wait_r_sends, 0)
+        )
+        out_ref[:, :, columns] = mixed.reshape(OWNER_SLOTS, STEPS, HEAD_SIZE).astype(BF16)
+    terms = three_terms(spread_terms(mass * (alive * LN2)))
+    by_step = one_hot(
+        (iota((SLOT_ROWS, SLOT_ROWS), 0) % STEPS == iota((SLOT_ROWS, SLOT_ROWS), 1) // OWNER_SLOTS)
+        & (iota((SLOT_ROWS, SLOT_ROWS), 0) // STEPS == iota((SLOT_ROWS, SLOT_ROWS), 1) % OWNER_SLOTS)
+    ).astype(BF16)
+    turned = lax.dot_general(terms, by_step, (((0,), (0,)), ((), ())), preferred_element_type=F32)
+    turned = turned[:GROUP] + turned[GROUP : 2 * GROUP] + turned[2 * GROUP : 3 * GROUP]
+    for t in range(STEPS):
+        mass_ref[t] = turned[:, t * OWNER_SLOTS : (t + 1) * OWNER_SLOTS]
+
+    for i in range(row_count - 1):
+        r_copy(i).wait_send()
+
+
+def hand_over(attended, mass, attended_out, mass_out):
+    attended_out[...] = attended[...]
+    mass_out[...] = mass[...]
 
 
 def per_device(probe_vectors, tail_memory, lead_memory, active_rollouts, holder_map, tail_fill):
     row_count = lax.axis_size("prompt")
     ctx_count = lax.axis_size("ctx")
+    x_count = ctx_count // 2
     slots, steps, width = probe_vectors.shape
     span = lead_memory.shape[1]
     tail_span = tail_memory.shape[1]
@@ -497,19 +604,26 @@
     attended, log_mass = pl.pallas_call(
         kernel,
         out_shape=(
-            jax.ShapeDtypeStruct((slots * steps, width), BF16),
-            jax.ShapeDtypeStruct((slots * steps, GROUP), F32),
+            jax.ShapeDtypeStruct((slots, steps, width), BF16),
+            jax.ShapeDtypeStruct((steps, GROUP, slots), F32),
         ),
-        in_specs=[vmem, vmem, vmem, vmem, anywhere, anywhere],
+        in_specs=[anywhere] * 6,
         out_specs=(vmem, vmem),
         scratch_shapes=[
+            pltpu.VMEM((slots, steps, width), BF16),
+            pltpu.VMEM((1, active_rollouts.shape[0]), jnp.int32),
+            pltpu.VMEM((1, holder_map.shape[0]), jnp.int32),
+            pltpu.VMEM((1, slots), jnp.int32),
             pltpu.VMEM((slots, tail_span, 2 * HEAD_SIZE), BF16),
             pltpu.VMEM((ctx_count, span, 2 * HEAD_SIZE), BF16),
+            pltpu.VMEM((SLOT_ROWS, WIDTH), BF16),
             pltpu.VMEM((pairs, WIDTH), BF16),
             pltpu.VMEM((pairs, WIDTH), BF16),
             pltpu.VMEM((ctx_count, ROWS, WIDTH), BF16),
             pltpu.VMEM((ctx_count, ROWS, PAYLOAD), BF16),
-            pltpu.VMEM((ctx_count, ROWS, PAYLOAD), BF16),
+            pltpu.VMEM((x_count, ROWS, PAYLOAD), BF16),
+            pltpu.VMEM((x_count, ROWS, PAYLOAD), BF16),
+            pltpu.VMEM((x_count, ROWS, PAYLOAD), BF16),
             pltpu.VMEM((pairs, PAYLOAD), BF16),
             pltpu.VMEM((pairs, PAYLOAD), BF16),
             pltpu.VMEM((SLOT_ROWS, WIDTH), F32),
@@ -517,14 +631,17 @@
             pltpu.VMEM((ROWS, pairs), BF16),
             pltpu.VMEM((pairs, ROWS), BF16),
             pltpu.VMEM((SLOT_ROWS, pairs), BF16),
+            dma((4,)),
             dma,
             dma((ctx_count,)),
             dma((row_count,)),
             dma((row_count,)),
             dma((ctx_count,)),
             dma((ctx_count,)),
-            dma((ctx_count,)),
-            dma((ctx_count,)),
+            dma((x_count,)),
+            dma((x_count,)),
+            dma((x_count,)),
+            dma((x_count,)),
             dma((row_count,)),
             dma((row_count,)),
         ],
@@ -536,14 +653,24 @@
         ),
         name="grouped_attention",
     )(
-        probe_vectors.reshape(slots * steps, width),
+        probe_vectors,
         active_rollouts.reshape(1, -1),
         holder_map.reshape(1, -1),
         tail_fill.reshape(1, -1),
         tail_memory,
         lead_memory.reshape(span, -1),
     )
-    return attended.reshape(slots, steps, width), log_mass.reshape(slots, steps, GROUP)
+    attended, log_mass = pl.pallas_call(
+        hand_over,
+        out_shape=(
+            jax.ShapeDtypeStruct(attended.shape, attended.dtype),
+            jax.ShapeDtypeStruct(log_mass.shape, log_mass.dtype),
+        ),
+        in_specs=[vmem, vmem],
+        out_specs=(vmem, vmem),
+        name="hand_over",
+    )(attended, log_mass)
+    return attended, jnp.transpose(log_mass, (2, 0, 1))
 
 
 def solution(mesh):

time: 52.5 us -> 44.6 us (0.85)
  the two profiles are of different devices: /device:TPU:2 before, /device:TPU:1 now
where the time goes in v2:
time: 44.6 us; the launch traced here: 44.5 us
  Pallas kernels  43.9 us (98%)
  between operations  0.64 us (1%)
    pallas_call x1, Pallas kernels, per_device(): pl.pallas_call(kernel, out_shape=(jax.ShapeDtypeStruct((slots, steps, wid...  42.3 us
    pallas_call x1, Pallas kernels, per_device(): pl.pallas_call(hand_over, out_shape=(jax.ShapeDtypeStruct(attended.shape,...  1.57 us

profile of v2, /device:TPU:1, one launch (start us, length us, event | category | flops | bytes accessed | tf_op | source)
XLA Modules:
  0.0 44.5 jit_solution(10110987001351632532)
XLA Ops:
  0.6 42.3 %grouped_attention.1 = (bf16[16,4,1024]{2,1,0:T(4,128)(2,1)}, f32[4,8,16]{2,1,0:T(8,128)}) custom-call(bf16[16,4,1024]{2,1,0:T(4,128)(2,1)} %probes_hbm.1, s32[1,16]{1,0:T(1,128)} %bitcast.6, s32[1,128]{1,0:T(1,128)} %bitcast.7, s32[1,16]{1,0:T(1,128)} %bitcast.8, bf16[16,512,256]{2,1,0:T(8,128)(2,1)} %tail_hbm.1, bf16[4096,2048]{1,0:T(8,128)(2,1)} %bitcast.5), custom_call_target="tpu_custom_call" | custom-call | flops 5000000000 | bytes 22000000 | tf_op jit(solution)/shard_map/grouped_attention/pallas_call | solution.py:604
  42.9 1.6 %hand_over.1 = (bf16[16,4,1024]{2,1,0:T(4,128)(2,1)}, f32[4,8,16]{2,1,0:T(8,128)}) custom-call(bf16[16,4,1024]{2,1,0:T(4,128)(2,1)} %get-tuple-element.6.attended, f32[4,8,16]{2,1,0:T(8,128)} %get-tuple-element.7.mass), custom_call_target="tpu_custom_call" | custom-call | tf_op jit(solution)/shard_map/hand_over/pallas_call | solution.py:663

commit v3 on v2

--- a/solution.py
+++ b/solution.py
@@ -21,8 +21,7 @@
 SLOT_ROWS = OWNER_SLOTS * STEPS
 PAIR_ROWS = CAP * STEPS
 CHUNK = 1024
-EARLY_GROUPS = 4
-LATE_GROUPS = 0
+EARLY_GROUPS = 3
 FINISH_STEP = 6
 LOG2E = 1.4426950408889634
 LN2 = 0.6931471805599453
@@ -149,9 +148,7 @@
     recv_q,
     heads_q,
     part_out,
-    twin_in,
-    pair_out,
-    pair_in,
+    part_in,
     ret_out,
     ret_in,
     suffix,
@@ -167,7 +164,6 @@
     c_send,
     c_recv,
     t_send,
-    t_recv,
     p_send,
     p_recv,
     r_send,
@@ -180,8 +176,8 @@
     z_count = row_count // y_count
     me = lax.axis_index("prompt")
     ctx = lax.axis_index("ctx")
-    x, core = ctx // 2, ctx % 2
-    z, y = me // y_count, me % y_count
+    x, core = lax.div(ctx, 2), lax.rem(ctx, 2)
+    z, y = lax.div(me, y_count), lax.rem(me, y_count)
     span = lead_hbm.shape[0]
     chunk = min(CHUNK, span)
     pairs = row_count * PAIR_ROWS
@@ -199,10 +195,10 @@
     )
 
     def row_peer(offset):
-        return ((z + offset[0]) % z_count) * y_count + (y + offset[1]) % y_count
+        return lax.rem(z + offset[0], z_count) * y_count + lax.rem(y + offset[1], y_count)
 
     def ctx_peer(offset):
-        return ((x + offset[0]) % x_count) * 2 + (core + offset[1]) % 2
+        return lax.rem(x + offset[0], x_count) * 2 + lax.rem(core + offset[1], 2)
 
     def pair_block(index):
         return pl.ds(pl.multiple_of(index * PAIR_ROWS, PAIR_ROWS), PAIR_ROWS)
@@ -223,14 +219,15 @@
         copy.start()
 
     def step_x(s):
-        return (x + s % x_count + s // x_count) % x_count
+        return lax.rem(x + lax.rem(s, x_count) + lax.div(s, x_count), x_count)
 
     def step_core(s):
-        return s // x_count
+        return lax.div(s, x_count)
 
     def step_head(s):
         return step_x(s) * 2 + step_core(s)
 
+    own_step = core * (ctx_count - 1)
     tail_copy = pltpu.make_async_copy(tail_hbm, tail, tail_sem)
     tail_copy.start()
 
@@ -370,9 +367,11 @@
         return 0
 
     groups = OWNER_SLOTS // batch
-    lax.fori_loop(0, EARLY_GROUPS, suffix_group, 0)
+    early = EARLY_GROUPS + (groups - EARLY_GROUPS) * core
+    lax.fori_loop(0, early, suffix_group, 0)
     pl.when(core == 1)(start_q)
-    lax.fori_loop(EARLY_GROUPS, groups - LATE_GROUPS, suffix_group, 0)
+
+    near = [(0, 1)] + [(x_count - k, 0) for k in range(1, x_count)]
 
     def c_copy(i):
         return pltpu.make_async_remote_copy(
@@ -380,15 +379,15 @@
             dst_ref=heads_q.at[ctx],
             send_sem=c_send.at[i],
             recv_sem=c_recv.at[ctx],
-            device_id={"ctx": ctx_peer(ctx_offsets[i])},
+            device_id={"ctx": ctx_peer(near[i])},
             device_id_type=MESH,
         )
 
-    def c_arrival(head):
+    def twin_copy(head):
         return pltpu.make_async_remote_copy(
             src_ref=heads_q.at[head],
             dst_ref=heads_q.at[head],
-            send_sem=c_send.at[0],
+            send_sem=t_send.at[head // 2],
             recv_sem=c_recv.at[head],
             device_id={"ctx": ctx_peer((0, 1))},
             device_id_type=MESH,
@@ -398,37 +397,26 @@
         for i in range(row_count - 1):
             q_copy(i).wait_recv()
         heads_q[ctx] = dot(take_table[...], recv_q[...]).astype(BF16)
-        for i in reversed(range(ctx_count - 1)):
+        for i in range(len(near)):
             c_copy(i).start()
 
-    def t_copy(j):
+    def p_copy(s):
         return pltpu.make_async_remote_copy(
-            src_ref=part_out.at[(1 - core) * x_count + j],
-            dst_ref=twin_in.at[j],
-            send_sem=t_send.at[j],
-            recv_sem=t_recv.at[j],
-            device_id={"ctx": ctx_peer((0, 1))},
+            src_ref=part_out.at[s],
+            dst_ref=part_in.at[ctx],
+            send_sem=p_send.at[s],
+            recv_sem=p_recv.at[ctx],
+            device_id={"ctx": step_head(s)},
             device_id_type=MESH,
         )
 
-    def p_copy(j):
+    def p_arrival(source):
         return pltpu.make_async_remote_copy(
-            src_ref=pair_out.at[j],
-            dst_ref=pair_in.at[x],
-            send_sem=p_send.at[j],
-            recv_sem=p_recv.at[x],
-            device_id={"ctx": step_x(core * x_count + j) * 2 + core},
-            device_id_type=MESH,
-        )
-
-    def p_arrival(offset):
-        source = (x + offset) % x_count
-        return pltpu.make_async_remote_copy(
-            src_ref=pair_out.at[0],
-            dst_ref=pair_in.at[source],
+            src_ref=part_out.at[0],
+            dst_ref=part_in.at[source],
             send_sem=p_send.at[0],
             recv_sem=p_recv.at[source],
-            device_id={"ctx": source * 2 + core},
+            device_id={"ctx": source},
             device_id_type=MESH,
         )
 
@@ -453,20 +441,6 @@
         merged.append(three_terms(spread_terms(highest + jnp.log2(whole))))
         return jnp.concatenate(merged, axis=1)
 
-    def merge_pair(s):
-        j = s % x_count
-        t_copy(j).wait_recv()
-        both = merge([part_out[s], twin_in[j]])
-
-        @pl.when(step_x(s) == x)
-        def _():
-            pair_in[x] = both
-
-        @pl.when(step_x(s) != x)
-        def _():
-            pair_out[j] = both
-            p_copy(j).start()
-
     def r_copy(i):
         peer = row_peer(row_offsets[i])
         return pltpu.make_async_remote_copy(
@@ -479,9 +453,10 @@
         )
 
     def finish_head():
-        for offset in range(1, x_count):
-            p_arrival(offset).wait_recv()
-        merged = merge([pair_in[i] for i in range(x_count)])
+        others = [ctx_peer(offset) for offset in ctx_offsets]
+        for other in others:
+            p_arrival(other).wait_recv()
+        merged = merge([part_out[own_step]] + [part_in[other] for other in others])
         ret_out[...] = dot(back_table[...], merged).astype(BF16)
         for i in range(row_count - 1):
             r_copy(i).start()
@@ -515,28 +490,27 @@
         pl.when(s == core)(take_queries)
         lead_copy(s).wait()
 
-        @pl.when(step_head(s) != ctx)
+        ahead = s + core
+
+        @pl.when((step_core(ahead) == core) & (ahead != own_step))
         def _():
-            c_arrival(step_head(s)).wait_recv()
-
-        prefix_head(s)
-        j = s % x_count
+            handed = twin_copy(step_head(ahead))
+            handed.wait_recv()
+            handed.start()
 
         @pl.when(step_core(s) != core)
         def _():
-            t_copy(j).start()
-
-        merged_step = s - 1 + core
-
-        @pl.when((merged_step >= core * x_count) & (merged_step < (core + 1) * x_count))
+            twin_copy(step_head(s)).wait_recv()
+
+        prefix_head(s)
+
+        @pl.when(s != own_step)
         def _():
-            merge_pair(merged_step)
-
-        if LATE_GROUPS:
-
-            @pl.when(s == 0)
-            def _():
-                lax.fori_loop(groups - LATE_GROUPS, groups, suffix_group, 0)
+            p_copy(s).start()
+
+        @pl.when(s == 0)
+        def _():
+            lax.fori_loop(early, groups, suffix_group, 0)
 
         pl.when(s == FINISH_STEP + (ctx_count - 1 - FINISH_STEP) * core)(finish_head)
         return 0
@@ -545,14 +519,15 @@
 
     for i in range(row_count - 1):
         q_copy(i).wait_send()
-    for i in range(ctx_count - 1):
+    for i in range(len(near)):
         c_copy(i).wait_send()
-    for j in range(x_count):
-        t_copy(j).wait_send()
-
-        @pl.when(step_x(core * x_count + j) != x)
+    for k in range(1, x_count):
+        twin_copy((x + k) % x_count * 2 + core).wait_send()
+    for s in range(ctx_count):
+
+        @pl.when(s != own_step)
         def _():
-            p_copy(j).wait_send()
+            p_copy(s).wait_send()
 
     for i in range(row_count - 1):
         r_copy(i).wait_recv()
@@ -593,7 +568,6 @@
 def per_device(probe_vectors, tail_memory, lead_memory, active_rollouts, holder_map, tail_fill):
     row_count = lax.axis_size("prompt")
     ctx_count = lax.axis_size("ctx")
-    x_count = ctx_count // 2
     slots, steps, width = probe_vectors.shape
     span = lead_memory.shape[1]
     tail_span = tail_memory.shape[1]
@@ -621,9 +595,7 @@
             pltpu.VMEM((pairs, WIDTH), BF16),
             pltpu.VMEM((ctx_count, ROWS, WIDTH), BF16),
             pltpu.VMEM((ctx_count, ROWS, PAYLOAD), BF16),
-            pltpu.VMEM((x_count, ROWS, PAYLOAD), BF16),
-            pltpu.VMEM((x_count, ROWS, PAYLOAD), BF16),
-            pltpu.VMEM((x_count, ROWS, PAYLOAD), BF16),
+            pltpu.VMEM((ctx_count, ROWS, PAYLOAD), BF16),
             pltpu.VMEM((pairs, PAYLOAD), BF16),
             pltpu.VMEM((pairs, PAYLOAD), BF16),
             pltpu.VMEM((SLOT_ROWS, WIDTH), F32),
@@ -638,10 +610,9 @@
             dma((row_count,)),
             dma((ctx_count,)),
             dma((ctx_count,)),
-            dma((x_count,)),
-            dma((x_count,)),
-            dma((x_count,)),
-            dma((x_count,)),
+            dma((ctx_count // 2,)),
+            dma((ctx_count,)),
+            dma((ctx_count,)),
             dma((row_count,)),
             dma((row_count,)),
         ],

time: 44.6 us -> 43.6 us (0.978)
  Pallas kernels: 43.9 us -> 42.9 us
    pallas_call x1, Pallas kernels: 42.3 us -> 41.3 us  [per_device(): pl.pallas_call(kernel, out_shape=(jax.ShapeDtypeStruct((slots, steps, wid...]
where the time goes in v3:
time: 43.6 us; the launch traced here: 43.5 us
  Pallas kernels  42.9 us (98%)
  between operations  0.64 us (1%)
    pallas_call x1, Pallas kernels, per_device(): pl.pallas_call(kernel, out_shape=(jax.ShapeDtypeStruct((slots, steps, wid...  41.3 us
    pallas_call x1, Pallas kernels, per_device(): pl.pallas_call(hand_over, out_shape=(jax.ShapeDtypeStruct(attended.shape,...  1.57 us

profile of v3, /device:TPU:1, one launch (start us, length us, event | category | flops | bytes accessed | tf_op | source)
XLA Modules:
  0.0 43.5 jit_solution(12367837133098243582)
XLA Ops:
  0.6 41.3 %grouped_attention.1 = (bf16[16,4,1024]{2,1,0:T(4,128)(2,1)}, f32[4,8,16]{2,1,0:T(8,128)}) custom-call(bf16[16,4,1024]{2,1,0:T(4,128)(2,1)} %probes_hbm.1, s32[1,16]{1,0:T(1,128)} %bitcast.6, s32[1,128]{1,0:T(1,128)} %bitcast.7, s32[1,16]{1,0:T(1,128)} %bitcast.8, bf16[16,512,256]{2,1,0:T(8,128)(2,1)} %tail_hbm.1, bf16[4096,2048]{1,0:T(8,128)(2,1)} %bitcast.5), custom_call_target="tpu_custom_call" | custom-call | flops 5000000000 | bytes 22000000 | tf_op jit(solution)/shard_map/grouped_attention/pallas_call | solution.py:578
  41.9 1.6 %hand_over.1 = (bf16[16,4,1024]{2,1,0:T(4,128)(2,1)}, f32[4,8,16]{2,1,0:T(8,128)}) custom-call(bf16[16,4,1024]{2,1,0:T(4,128)(2,1)} %get-tuple-element.6.attended, f32[4,8,16]{2,1,0:T(8,128)} %get-tuple-element.7.mass), custom_call_target="tpu_custom_call" | custom-call | tf_op jit(solution)/shard_map/hand_over/pallas_call | solution.py:634

commit v4 on v3

--- a/solution.py
+++ b/solution.py
@@ -135,8 +135,10 @@
     fill_hbm,
     tail_hbm,
     lead_hbm,
-    out_ref,
-    mass_ref,
+    ret_in,
+    suffix_hbm,
+    suffix_lse_hbm,
+    home_table_hbm,
     probes,
     active,
     holder,
@@ -150,7 +152,6 @@
     part_out,
     part_in,
     ret_out,
-    ret_in,
     suffix,
     suffix_lse,
     take_table,
@@ -168,6 +169,8 @@
     p_recv,
     r_send,
     r_recv,
+    own_sem,
+    home_sem,
 ):
     row_count = lax.axis_size("prompt")
     ctx_count = lax.axis_size("ctx")
@@ -331,6 +334,13 @@
     block_rows = batch * STEPS
     tail_rows = GROUP * block_rows
     tail_span = tail.shape[1]
+
+    home_copies = [
+        pltpu.make_async_copy(source, target, home_sem.at[i])
+        for i, (source, target) in enumerate(
+            [(suffix, suffix_hbm), (suffix_lse, suffix_lse_hbm), (home_table, home_table_hbm)]
+        )
+    ]
 
     def suffix_group(q, _):
         rows = pl.ds(pl.multiple_of(q * block_rows, block_rows), block_rows)
@@ -452,6 +462,9 @@
             device_id_type=MESH,
         )
 
+    def own_copy():
+        return pltpu.make_async_copy(ret_out.at[pair_block(me)], ret_in.at[pair_block(me)], own_sem)
+
     def finish_head():
         others = [ctx_peer(offset) for offset in ctx_offsets]
         for other in others:
@@ -460,7 +473,7 @@
         ret_out[...] = dot(back_table[...], merged).astype(BF16)
         for i in range(row_count - 1):
             r_copy(i).start()
-        ret_in[pair_block(me), :] = ret_out[pair_block(me), :]
+        own_copy().start()
 
     def prefix_head(s):
         query = split_query(heads_q[step_head(s)])
@@ -511,6 +524,8 @@
         @pl.when(s == 0)
         def _():
             lax.fori_loop(early, groups, suffix_group, 0)
+            for copy in home_copies:
+                copy.start()
 
         pl.when(s == FINISH_STEP + (ctx_count - 1 - FINISH_STEP) * core)(finish_head)
         return 0
@@ -531,9 +546,18 @@
 
     for i in range(row_count - 1):
         r_copy(i).wait_recv()
-
-    home = dot(home_table[...], ret_in[...])
-    alive = jnp.sum(home_table[...].astype(F32), axis=1, keepdims=True)
+    own_copy().wait()
+    for copy in home_copies:
+        copy.wait()
+
+    for i in range(row_count - 1):
+        r_copy(i).wait_send()
+
+
+def home_kernel(arrived, home_table, suffix, suffix_lse, out_ref, mass_ref):
+    table = home_table[...]
+    home = dot(table, arrived[...])
+    alive = jnp.sum(table.astype(F32), axis=1, keepdims=True)
     prefix_mass = sum_terms(home[:, WIDTH:])
     suffix_mass = suffix_lse[...]
     top = jnp.maximum(prefix_mass, suffix_mass)
@@ -556,14 +580,6 @@
     for t in range(STEPS):
         mass_ref[t] = turned[:, t * OWNER_SLOTS : (t + 1) * OWNER_SLOTS]
 
-    for i in range(row_count - 1):
-        r_copy(i).wait_send()
-
-
-def hand_over(attended, mass, attended_out, mass_out):
-    attended_out[...] = attended[...]
-    mass_out[...] = mass[...]
-
 
 def per_device(probe_vectors, tail_memory, lead_memory, active_rollouts, holder_map, tail_fill):
     row_count = lax.axis_size("prompt")
@@ -575,14 +591,16 @@
     vmem = pl.BlockSpec(memory_space=pltpu.VMEM)
     anywhere = pl.BlockSpec(memory_space=pl.ANY)
     dma = pltpu.SemaphoreType.DMA
-    attended, log_mass = pl.pallas_call(
+    arrived, suffix, suffix_lse, home_table = pl.pallas_call(
         kernel,
         out_shape=(
-            jax.ShapeDtypeStruct((slots, steps, width), BF16),
-            jax.ShapeDtypeStruct((steps, GROUP, slots), F32),
+            jax.ShapeDtypeStruct((pairs, PAYLOAD), BF16),
+            jax.ShapeDtypeStruct((SLOT_ROWS, WIDTH), F32),
+            jax.ShapeDtypeStruct((SLOT_ROWS, 128), F32),
+            jax.ShapeDtypeStruct((SLOT_ROWS, pairs), BF16),
         ),
         in_specs=[anywhere] * 6,
-        out_specs=(vmem, vmem),
+        out_specs=(anywhere,) * 4,
         scratch_shapes=[
             pltpu.VMEM((slots, steps, width), BF16),
             pltpu.VMEM((1, active_rollouts.shape[0]), jnp.int32),
@@ -596,7 +614,6 @@
             pltpu.VMEM((ctx_count, ROWS, WIDTH), BF16),
             pltpu.VMEM((ctx_count, ROWS, PAYLOAD), BF16),
             pltpu.VMEM((ctx_count, ROWS, PAYLOAD), BF16),
-            pltpu.VMEM((pairs, PAYLOAD), BF16),
             pltpu.VMEM((pairs, PAYLOAD), BF16),
             pltpu.VMEM((SLOT_ROWS, WIDTH), F32),
             pltpu.VMEM((SLOT_ROWS, 128), F32),
@@ -615,6 +632,8 @@
             dma((ctx_count,)),
             dma((row_count,)),
             dma((row_count,)),
+            dma,
+            dma((3,)),
         ],
         compiler_params=pltpu.CompilerParams(
             collective_id=0, has_side_effects=True, vmem_limit_bytes=56 * 2**20
@@ -632,15 +651,15 @@
         lead_memory.reshape(span, -1),
     )
     attended, log_mass = pl.pallas_call(
-        hand_over,
+        home_kernel,
         out_shape=(
-            jax.ShapeDtypeStruct(attended.shape, attended.dtype),
-            jax.ShapeDtypeStruct(log_mass.shape, log_mass.dtype),
+            jax.ShapeDtypeStruct((slots, steps, width), BF16),
+            jax.ShapeDtypeStruct((steps, GROUP, slots), F32),
         ),
-        in_specs=[vmem, vmem],
+        in_specs=[vmem] * 4,
         out_specs=(vmem, vmem),
-        name="hand_over",
-    )(attended, log_mass)
+        name="home_rows",
+    )(arrived, home_table, suffix, suffix_lse)
     return attended, jnp.transpose(log_mass, (2, 0, 1))
 
 

time: 43.6 us -> 43.4 us (level)
  no operation moved by 1% of the time
where the time goes in v4:
time: 43.4 us; the launch traced here: 43.3 us
  Pallas kernels  42.7 us (98%)
  between operations  0.64 us (1%)
    pallas_call x1, Pallas kernels, per_device(): pl.pallas_call(kernel, out_shape=(jax.ShapeDtypeStruct((pairs, PAYLOAD),...  40.2 us
    pallas_call x1, Pallas kernels, per_device(): pl.pallas_call(home_kernel, out_shape=(jax.ShapeDtypeStruct((slots, steps...  2.42 us

profile of v4, /device:TPU:1, one launch (start us, length us, event | category | flops | bytes accessed | tf_op | source)
XLA Modules:
  0.0 43.3 jit_solution(5608635955026502060)
XLA Ops:
  0.6 40.2 %grouped_attention.1 = (bf16[256,1152]{1,0:T(8,128)(2,1)}, f32[64,1024]{1,0:T(8,128)}, f32[64,128]{1,0:T(8,128)}, bf16[64,256]{1,0:T(8,128)(2,1)}) custom-call(bf16[16,4,1024]{2,1,0:T(4,128)(2,1)} %probes_hbm.1, s32[1,16]{1,0:T(1,128)} %bitcast.6, s32[1,128]{1,0:T(1,128)} %bitcast.7, s32[1,16]{1,0:T(1,128)} %bitcast.8, bf16[16,512,256]{2,1,0:T(8,128)(2,1)} %tail_hbm.1, ...), custom_call_target="tpu_custom_call" | custom-call | flops 5000000000 | bytes 22000000 | tf_op jit(solution)/shard_map/grouped_attention/pallas_call | solution.py:594
  40.9 2.4 %home_rows.1 = (bf16[16,4,1024]{2,1,0:T(4,128)(2,1)}, f32[4,8,16]{2,1,0:T(8,128)}) custom-call(bf16[256,1152]{1,0:T(8,128)(2,1)} %get-tuple-element.8.arrived, bf16[64,256]{1,0:T(8,128)(2,1)} %get-tuple-element.9.home_table, f32[64,1024]{1,0:T(8,128)} %get-tuple-element.10.suffix, f32[64,128]{1,0:T(8,128)} %get-tuple-element.11.suffix_lse), custom_call_target="tpu_custom_call" | custom-call | tf_op jit(solution)/shard_map/home_rows/pallas_call | solution.py:653
